TPU v7x, 32 devices: a whole 2x2x4 slice. The times are simulated.
32 devices in a mesh: xy: 8 (over z, y), gz: 4 (over x, core).
Axes of the slice: x: 2, y: 2, z: 4, core: 2. Of those that a mesh axis runs over, the one named last changes fastest.
Arguments:
- base_field: bfloat16 [132, 32, 32, 256], P(None, 'gz', 'xy'), may hold values from 0 to 2
- increments: bfloat16 [132, 262144], P(None, ('xy', 'gz')), may hold values from -6 to 6
- dest_tile: int32 [262144, 1], P(('xy', 'gz')), may hold values from 0 to 7; in each aligned block of 8192 rows (0 to 8191, 8192 to 16383, ...) at most 2048 rows name the same one
- dest_cell: int32 [262144], P(('xy', 'gz')), may hold values from 0 to 8191
- courant_x: bfloat16 [32, 32, 256], P('gz', 'xy'), may hold values from -0.23925781 to 0.23925781
- courant_y: bfloat16 [32, 32, 256], P('gz', 'xy'), may hold values from -0.23925781 to 0.23925781
- fall_courant: float32 [132, 32], replicated, may hold values from 0.001 to 280
Outputs:
- settled: bfloat16 [132, 32, 32, 256], P(None, 'gz', 'xy')
Inputs may be any that keep to these rules, and one draw needn't show every extreme that they name: `dest_tile`: among the rows of one device, at most 2048 name the same tile; in every draw some device has exactly 2048 rows naming one tile.
All inputs are finite; a program needn't handle non-finite values.
Results may differ from a plain program's by a relative error of at most 0.0043.
Values may be sent and summed in bfloat16 or wider, within the bound.
A program may use at most 128 MiB of HBM per device.

v0:
```python
import functools

import jax
import jax.numpy as jnp
from jax import lax
from jax.experimental import pallas as pl
from jax.experimental.pallas import tpu as pltpu
from jax.sharding import PartitionSpec as P

MESH = pl.DeviceIdType.MESH
NT = (((1,), (1,)), ((), ()))
TAIL = 16


def one_hot(condition):
    return jnp.where(condition, 1.0, 0.0).astype(jnp.bfloat16)


def stages_of(body):
    parts = [(body, TAIL)]
    first = 0
    while first < body:
        rows = 16 if body - first <= 32 else 32
        parts.append((first, rows))
        first += rows
    return parts


def pack_kernel(
    peers, capacity, inc, tiles, cells, main_out, tail_out, packed, tails, places, starts, table, sem, out_sem
):
    comps, count = inc.shape
    body = comps // 16 * 16
    height = body + TAIL
    run, width = 128, 256
    lines = count // run
    half = capacity // 2

    def clear(tile, carry):
        packed[tile] = jnp.zeros(packed.shape[1:], packed.dtype)
        return carry

    lax.fori_loop(0, peers, clear, 0)

    ahead = one_hot(
        lax.broadcasted_iota(jnp.int32, (run, run), 0) <= lax.broadcasted_iota(jnp.int32, (run, run), 1)
    )
    every = jnp.ones((run, run), jnp.bfloat16)
    above = one_hot(
        lax.broadcasted_iota(jnp.int32, (lines, lines), 0)
        > lax.broadcasted_iota(jnp.int32, (lines, lines), 1)
    )
    lanes = lax.broadcasted_iota(jnp.int32, (lines, run), 1)
    bundle = min(8, peers)

    def rank(part, carry):
        place, start = carry
        for n in range(bundle):
            tile = part * bundle + n
            member = jnp.where(tiles[...] == tile, 1.0, 0.0)
            taken = member.astype(jnp.bfloat16)
            inside = jnp.dot(taken, ahead, preferred_element_type=jnp.float32)
            line = jnp.dot(taken, every, preferred_element_type=jnp.float32).astype(jnp.bfloat16)
            before = jnp.dot(above, line, preferred_element_type=jnp.float32)
            place = place + member * (inside + before - 1.0)
            start = start + jnp.where(lanes == tile, before, 0.0)
        return place, start

    zero = jnp.zeros((lines, run), jnp.float32)
    place, start = lax.fori_loop(0, peers // bundle, rank, (zero, zero))
    places[...] = place.astype(jnp.int32) % width
    starts[...] = start.astype(jnp.int32)
    copy = pltpu.make_async_copy(starts, table, sem)
    copy.start()
    copy.wait()

    window = lax.broadcasted_iota(jnp.int32, (width, width), 0)
    lane = lax.broadcasted_iota(jnp.int32, (16, width), 1)
    sub = lax.broadcasted_iota(jnp.int32, (8, width), 0)

    def pair(ref, block):
        return jnp.concatenate([ref[pl.ds(2 * block, 1)], ref[pl.ds(2 * block + 1, 1)]], axis=1)

    def step(block, carry):
        columns = pl.ds(pl.multiple_of(block * width, width), width)
        match = one_hot(window == pair(places, block))
        owner = pair(tiles, block)
        cell = pair(cells, block)
        extra = jnp.concatenate(
            [inc[body:comps, columns].astype(jnp.float32), jnp.zeros((8 - comps + body, width), jnp.float32)],
            axis=0,
        )
        extra = jnp.where(sub == 4, (cell % width).astype(jnp.float32), extra)
        extra = jnp.where(sub == 5, (cell // width).astype(jnp.float32), extra)
        extra = jnp.concatenate([extra, jnp.zeros((8, width), jnp.float32)], axis=0)
        rows = jnp.concatenate([inc[0:body, columns], extra.astype(jnp.bfloat16)], axis=0)

        def place_part(part, inner):
            first = part * bundle
            masked = jnp.concatenate(
                [rows * one_hot(owner == first + n) for n in range(bundle)], axis=0
            )
            moved = lax.dot_general(masked, match, NT, preferred_element_type=jnp.float32)
            for n in range(bundle):
                tile = first + n
                begin = table[2 * block, tile]
                chunk, low = begin // width, begin % width
                value = moved[n * height : (n + 1) * height].astype(jnp.bfloat16)
                now = one_hot(lane >= low)
                later = one_hot(lane < low)
                here = pl.ds(pl.multiple_of(chunk * width, width), width)
                there = pl.ds(pl.multiple_of(chunk * width + width, width), width)
                now = jnp.concatenate([now] * (height // 16), axis=0)
                later = jnp.concatenate([later] * (height // 16), axis=0)
                packed[tile, :, here] += value * now
                packed[tile, :, there] = value * later
            return inner

        lax.fori_loop(0, peers // bundle, place_part, 0)
        return carry

    lax.fori_loop(0, count // width, step, 0)

    def out_copy(tile):
        return pltpu.make_async_copy(
            packed.at[tile, 0:body, 0:capacity], main_out.at[tile], out_sem.at[tile]
        )

    def leave(tile, carry):
        out_copy(tile).start()
        left = packed[tile, body:height, 0:half].astype(jnp.float32)[0:8]
        right = packed[tile, body:height, half:capacity].astype(jnp.float32)[0:8]
        tails[tile] = jnp.concatenate([left, right], axis=0).astype(jnp.bfloat16)
        return carry

    lax.fori_loop(0, peers, leave, 0)
    copy = pltpu.make_async_copy(tails, tail_out, sem)
    copy.start()

    def left_all(tile, carry):
        out_copy(tile).wait()
        return carry

    lax.fori_loop(0, peers, left_all, 0)
    copy.wait()


def main_kernel(
    comps, ahead, packed, tails, base_in, cx, cy, fall, out, arrived, arrived_tail, cell_of, base, total,
    updated, advected, left, right, next_cx, flow, inflow, scale, gain, weight, face, send_sem, recv_sem,
    halo_send, halo_recv, face_send, face_recv, flow_send, flow_recv, own_sem,
):
    peers, body, capacity = packed.shape
    xcells, levels, height, width = updated.shape
    slabs = lax.axis_size("gz")
    me, slab = lax.axis_index("xy"), lax.axis_index("gz")
    has_prev, has_next = me > 0, me < peers - 1
    groups = xcells * levels
    stages = stages_of(body)
    half = capacity // 2

    own_main = pltpu.make_async_copy(packed.at[me], arrived.at[0], own_sem.at[0])
    own_tail = pltpu.make_async_copy(tails.at[me], arrived_tail.at[0], own_sem.at[1])
    base_copy = pltpu.make_async_copy(base_in, base, own_sem.at[2])
    own_tail.start()
    own_main.start()
    base_copy.start()

    barrier = pltpu.get_barrier_semaphore()

    def greet(step, carry):
        pl.semaphore_signal(
            barrier, inc=1, device_id=((me + step) % peers, slab), device_id_type=MESH
        )
        return carry

    lax.fori_loop(1, peers, greet, 0)
    for step in range(1, slabs):
        pl.semaphore_signal(
            barrier, inc=1, device_id=(me, (slab + step) % slabs), device_id_type=MESH
        )
    pl.semaphore_wait(barrier, peers - 1 + slabs - 1)

    def row_copy(number, step):
        first, rows = stages[number]
        target = (me + step) % peers
        if number == 0:
            source, landing = tails.at[target], arrived_tail.at[step]
        else:
            source = packed.at[target, pl.ds(first, rows)]
            landing = arrived.at[step, pl.ds(first, rows)]
        return pltpu.make_async_remote_copy(
            src_ref=source,
            dst_ref=landing,
            send_sem=send_sem.at[number, step],
            recv_sem=recv_sem.at[number, step],
            device_id=(target, slab),
            device_id_type=MESH,
        )

    def turn(order):
        away = order // 2
        return jnp.where(order % 2 == 0, peers // 2 + away, peers // 2 - 1 - away)

    def start_rows(number):
        def start(order, carry):
            row_copy(number, turn(order)).start()
            return carry

        lax.fori_loop(0, peers - 1, start, 0)

    for number in range(min(ahead, len(stages))):
        start_rows(number)

    face_to_prev = pltpu.make_async_remote_copy(
        src_ref=cx.at[0],
        dst_ref=next_cx,
        send_sem=face_send,
        recv_sem=face_recv,
        device_id=((me + peers - 1) % peers, slab),
        device_id_type=MESH,
    )

    @pl.when(has_prev)
    def _():
        face_to_prev.start()

    @pl.when(jnp.logical_not(has_prev))
    def _():
        left[...] = jnp.zeros_like(left)

    @pl.when(jnp.logical_not(has_next))
    def _():
        right[...] = jnp.zeros_like(right)
        next_cx[...] = jnp.zeros_like(next_cx)

    column = lax.broadcasted_iota(jnp.int32, (1, fall.shape[1]), 1)

    def along(values, at):
        picked = jnp.sum(jnp.where(column == at, values, 0.0), axis=1, keepdims=True)
        return jnp.broadcast_to(picked, (values.shape[0], 128))

    for first, rows, filled in ((0, body, body), (body, TAIL, comps - body)):
        rates = fall[first : first + filled]
        if filled < rows:
            rates = jnp.concatenate([rates, jnp.zeros((8 - filled, fall.shape[1]), jnp.float32)], axis=0)
            spare = jnp.zeros((rows - 8, 128), jnp.float32)
        divided = 1.0 / (1.0 + rates)
        kept = rates / (1.0 + rates)

        def put(ref, at, value):
            if filled < rows:
                value = jnp.concatenate([value, spare], axis=0)
            ref[at, first : first + rows] = value

        def coefficients(k, carry):
            put(scale, k, along(divided, slab * levels + k))
            put(gain, k, along(kept, slab * levels + k))
            return carry

        lax.fori_loop(0, levels, coefficients, 0)
        passed = jnp.ones((kept.shape[0], 128), jnp.float32)
        put(weight, 0, passed)
        for d in range(1, slabs - 1):

            def through(k, value):
                return value * along(kept, (slab + d) * levels + k)

            passed = lax.fori_loop(0, levels, through, passed)
            put(weight, d, passed)

    lane_cells = lax.broadcasted_iota(jnp.int32, (width, capacity), 0).astype(jnp.float32)

    def wide(value):
        return jnp.concatenate([value] * (width // 128), axis=1)

    def add_rows(number, step, begin):
        first, rows = stages[number]
        bundle = min(groups, 1024 // rows)
        if number == 0:
            block = arrived_tail[step].astype(jnp.float32)
            block = jnp.concatenate([block[0:8], block[8:16]], axis=1)
            cell_of[step] = block
            block = jnp.concatenate([block, jnp.zeros_like(block)], axis=0).astype(jnp.bfloat16)
        else:
            block = arrived[step, first : first + rows]
        low = cell_of[step, 4:5]
        high = cell_of[step, 5:6]
        match = one_hot(lane_cells == low)

        def product(part, inner):
            at = part * bundle
            masked = jnp.concatenate(
                [block * one_hot(high == (at + n).astype(jnp.float32)) for n in range(bundle)], axis=0
            )
            sums = lax.dot_general(masked, match, NT, preferred_element_type=jnp.float32)
            sums = sums.reshape(bundle, rows, width)
            if begin and number > 0:
                total[pl.ds(at, bundle), first : first + rows] = sums + base[
                    pl.ds(at, bundle), first : first + rows
                ].astype(jnp.float32)
            elif begin:
                total[pl.ds(at, bundle), first : first + rows] = sums
            else:
                total[pl.ds(at, bundle), first : first + rows] += sums
            return inner

        lax.fori_loop(0, groups // bundle, product, 0)

    def halo_copy(number, which):
        first, rows = stages[number]
        source = updated.at[xcells - 1 if which == 0 else 0, :, pl.ds(first, rows)]
        landing = (left if which == 0 else right).at[:, pl.ds(first, rows)]
        return pltpu.make_async_remote_copy(
            src_ref=source,
            dst_ref=landing,
            send_sem=halo_send.at[number, which],
            recv_sem=halo_recv.at[number, which],
            device_id=((me + (1 if which == 0 else peers - 1)) % peers, slab),
            device_id_type=MESH,
        )

    def finish(number):
        first, rows = stages[number]
        span = slice(first, first + rows)

        def group(counter, carry):
            value = total[counter, span]
            if number == 0:
                value = jnp.concatenate(
                    [
                        value[: comps - body] + base[counter, body:comps].astype(jnp.float32),
                        jnp.zeros((rows - comps + body, width), jnp.float32),
                    ],
                    axis=0,
                )
            updated[counter % xcells, counter // xcells, span] = value.astype(jnp.bfloat16)
            return carry

        lax.fori_loop(0, groups, group, 0, unroll=4)

        @pl.when(has_next)
        def _():
            halo_copy(number, 0).start()

        @pl.when(has_prev)
        def _():
            halo_copy(number, 1).start()

    def flow_copy(number, d):
        first, rows = stages[number]
        return pltpu.make_async_remote_copy(
            src_ref=flow.at[:, pl.ds(first, rows)],
            dst_ref=inflow.at[d - 1, :, pl.ds(first, rows)],
            send_sem=flow_send.at[number, d - 1],
            recv_sem=flow_recv.at[number, d - 1],
            device_id=(me, (slab + slabs - d) % slabs),
            device_id_type=MESH,
        )

    def faces():
        @pl.when(has_next)
        def _():
            face_to_prev.wait_recv()

        for i in range(xcells):
            west, south = cx[i], cy[i]
            east = next_cx[...] if i == xcells - 1 else cx[i + 1]
            north = pltpu.roll(south, width - 1, 1)
            face[0, i] = (
                1.0
                - (jnp.maximum(east, 0.0) - jnp.minimum(west, 0.0))
                - (jnp.maximum(north, 0.0) - jnp.minimum(south, 0.0))
            )
            face[1, i] = jnp.maximum(west, 0.0)
            face[2, i] = -jnp.minimum(east, 0.0)
            face[3, i] = jnp.maximum(south, 0.0)
            face[4, i] = -jnp.minimum(north, 0.0)

    def spans(number):
        first, rows = stages[number]
        return [slice(at, at + 16) for at in range(first, first + rows, 16)]

    def advect(number):
        def cells(chosen, span):
            def level(counter, flows):
                k = levels - 1 - counter
                row = pl.ds(k, 1)
                wanted = sorted({i + d for i in chosen for d in (-1, 0, 1)})
                layer = {}
                for i in wanted:
                    ref = left[k, span] if i < 0 else right[k, span] if i == xcells else updated[i, k, span]
                    layer[i] = ref.astype(jnp.float32)
                kept = wide(gain[k, span])
                result = []
                for i, flowing in zip(chosen, flows):
                    current = layer[i]
                    value = (
                        current * face[0, i, row]
                        + layer[i - 1] * face[1, i, row]
                        + layer[i + 1] * face[2, i, row]
                        + pltpu.roll(current, 1, 1) * face[3, i, row]
                        + pltpu.roll(current, width - 1, 1) * face[4, i, row]
                    ).astype(jnp.bfloat16)
                    advected[i, k, span] = value
                    result.append((value.astype(jnp.float32) + flowing) * kept)
                return tuple(result)

            none = tuple(jnp.zeros((16, width), jnp.float32) for _ in chosen)
            flows = lax.fori_loop(0, levels, level, none, unroll=2)
            for i, flowing in zip(chosen, flows):
                flow[i, span] = flowing

        inner = list(range(1, xcells - 1))
        for span in spans(number):
            cells(inner, span)

        @pl.when(has_prev)
        def _():
            halo_copy(number, 0).wait_recv()

        @pl.when(has_next)
        def _():
            halo_copy(number, 1).wait_recv()

        for span in spans(number):
            cells([0, xcells - 1], span)
        for d in range(1, slabs):

            @pl.when(slab >= d)
            def _(d=d):
                flow_copy(number, d).start()

    def settle(number):
        @pl.when(slab == slabs - 1)
        def _():
            for i in range(xcells):
                for span in spans(number):
                    inflow[0, i, span] = jnp.zeros((16, width), jnp.float32)

        for d in range(1, slabs):

            @pl.when(slab + d < slabs)
            def _(d=d):
                flow_copy(number, d).wait_recv()
                if d > 1:
                    for i in range(xcells):
                        for span in spans(number):
                            inflow[0, i, span] += wide(weight[d - 1, span]) * inflow[d - 1, i, span]

        for span in spans(number):
            filled = min(comps, span.stop) - span.start

            def level(counter, flows):
                k = levels - 1 - counter
                kept, divided = wide(gain[k, span]), wide(scale[k, span])
                result = []
                for i, flowing in enumerate(flows):
                    value = advected[i, k, span].astype(jnp.float32) + flowing
                    done = (value * divided).astype(jnp.bfloat16)
                    out[k * xcells + i, span.start : span.start + filled] = done[:filled]
                    result.append(value * kept)
                return tuple(result)

            start = tuple(inflow[0, i, span] for i in range(xcells))
            lax.fori_loop(0, levels, level, start, unroll=2)

    own_tail.wait()
    faces()
    for number in range(len(stages)):
        if number + ahead < len(stages):
            start_rows(number + ahead)
        if number == 1:
            own_main.wait()
            base_copy.wait()
        add_rows(number, 0, True)
        if number == 1:
            finish(0)

        def receive(order, carry):
            step = turn(order)
            row_copy(number, step).wait_recv()
            add_rows(number, step, False)
            return carry

        middle = (peers - 1) // 2
        lax.fori_loop(0, middle, receive, 0)
        if number > 1:
            settle(number - 2)
        lax.fori_loop(middle, peers - 1, receive, 0)
        if number > 0:
            advect(number - 1)
        if number > 0:
            finish(number)
    settle(len(stages) - 2)
    advect(len(stages) - 1)
    settle(len(stages) - 1)

    for number in range(len(stages)):

        def sent(step, carry):
            row_copy(number, step).wait_send()
            return carry

        lax.fori_loop(1, peers, sent, 0)

        @pl.when(has_next)
        def _():
            halo_copy(number, 0).wait_send()

        @pl.when(has_prev)
        def _():
            halo_copy(number, 1).wait_send()

        for d in range(1, slabs):

            @pl.when(slab >= d)
            def _(d=d):
                flow_copy(number, d).wait_send()

    @pl.when(has_prev)
    def _():
        face_to_prev.wait_send()


def per_device(base_field, increments, dest_tile, dest_cell, courant_x, courant_y, fall_courant):
    comps, levels, xcells, ycells = base_field.shape
    row_count = increments.shape[1]
    peers, slabs = lax.axis_size("xy"), lax.axis_size("gz")
    capacity = 2 * row_count // peers
    body = comps // 16 * 16
    height = body + TAIL
    groups = levels * xcells
    count = len(stages_of(body))
    lines = row_count // 128

    vmem = pl.BlockSpec(memory_space=pltpu.VMEM)
    anywhere = pl.BlockSpec(memory_space=pl.ANY)
    packed, tails = pl.pallas_call(
        functools.partial(pack_kernel, peers, capacity),
        out_shape=(
            jax.ShapeDtypeStruct((peers, body, capacity), jnp.bfloat16),
            jax.ShapeDtypeStruct((peers, TAIL, capacity // 2), jnp.bfloat16),
        ),
        in_specs=[vmem] * 3,
        out_specs=(anywhere, anywhere),
        scratch_shapes=[
            pltpu.VMEM((peers, height, capacity + 256), jnp.bfloat16),
            pltpu.VMEM((peers, TAIL, capacity // 2), jnp.bfloat16),
            pltpu.VMEM((lines, 128), jnp.int32),
            pltpu.VMEM((lines, 128), jnp.int32),
            pltpu.SMEM((lines, 128), jnp.int32),
            pltpu.SemaphoreType.DMA,
            pltpu.SemaphoreType.DMA((peers,)),
        ],
        compiler_params=pltpu.CompilerParams(vmem_limit_bytes=48 * 2**20),
        name="pack_rows",
    )(increments, dest_tile.reshape(lines, 128), dest_cell.reshape(lines, 128))

    base = jnp.transpose(base_field, (1, 2, 0, 3)).reshape(groups, comps, ycells)
    first = jnp.logical_and(
        lax.axis_index("xy") == 0, jnp.arange(xcells)[:, None, None] == 0
    )
    face_x = jnp.where(first, 0.0, jnp.transpose(courant_x.astype(jnp.float32), (1, 0, 2)))
    face_y = jnp.transpose(courant_y.astype(jnp.float32), (1, 0, 2))
    face_y = jnp.where(jnp.arange(ycells)[None, None, :] == 0, 0.0, face_y)

    settled = pl.pallas_call(
        functools.partial(main_kernel, comps, 1),
        out_shape=jax.ShapeDtypeStruct((groups, comps, ycells), jnp.bfloat16),
        in_specs=[anywhere] * 3 + [vmem] * 3,
        out_specs=vmem,
        scratch_shapes=[
            pltpu.VMEM((peers, body, capacity), jnp.bfloat16),
            pltpu.VMEM((peers, TAIL, capacity // 2), jnp.bfloat16),
            pltpu.VMEM((peers, 8, capacity), jnp.float32),
            pltpu.VMEM((groups, comps, ycells), jnp.bfloat16),
            pltpu.VMEM((groups, height, ycells), jnp.float32),
            pltpu.VMEM((xcells, levels, height, ycells), jnp.bfloat16),
            pltpu.VMEM((xcells, levels, height, ycells), jnp.bfloat16),
            pltpu.VMEM((levels, height, ycells), jnp.bfloat16),
            pltpu.VMEM((levels, height, ycells), jnp.bfloat16),
            pltpu.VMEM((levels, ycells), jnp.float32),
            pltpu.VMEM((xcells, height, ycells), jnp.float32),
            pltpu.VMEM((slabs - 1, xcells, height, ycells), jnp.float32),
            pltpu.VMEM((levels, height, 128), jnp.float32),
            pltpu.VMEM((levels, height, 128), jnp.float32),
            pltpu.VMEM((slabs - 1, height, 128), jnp.float32),
            pltpu.VMEM((5, xcells, levels, ycells), jnp.float32),
            pltpu.SemaphoreType.DMA((count, peers)),
            pltpu.SemaphoreType.DMA((count, peers)),
            pltpu.SemaphoreType.DMA((count, 2)),
            pltpu.SemaphoreType.DMA((count, 2)),
            pltpu.SemaphoreType.DMA,
            pltpu.SemaphoreType.DMA,
            pltpu.SemaphoreType.DMA((count, slabs - 1)),
            pltpu.SemaphoreType.DMA((count, slabs - 1)),
            pltpu.SemaphoreType.DMA((3,)),
        ],
        compiler_params=pltpu.CompilerParams(
            vmem_limit_bytes=56 * 2**20, collective_id=0, has_side_effects=True
        ),
        name="exchange_advect_settle",
    )(packed, tails, base, face_x, face_y, fall_courant)
    settled = settled.reshape(levels, xcells, comps, ycells)
    return jnp.transpose(settled, (2, 0, 1, 3))


def solution(mesh):
    in_specs = (
        P(None, "gz", "xy", None),
        P(None, ("xy", "gz")),
        P(("xy", "gz"), None),
        P(("xy", "gz")),
        P("gz", "xy", None),
        P("gz", "xy", None),
        P(),
    )
    out_specs = P(None, "gz", "xy", None)
    return jax.shard_map(
        per_device, mesh=mesh, in_specs=in_specs, out_specs=out_specs, check_vma=False
    )
```

profile of v0, /device:TPU:0, one launch (start us, length us, event | category | flops | bytes accessed | tf_op | source)
XLA Modules:
  0.0 165.2 jit_solution(1113728519595084633)
XLA Ops:
  0.0 1.4 select_bitcast_fusion
  1.4 0.0 copy-start
  1.4 0.0 copy-start.2
  1.4 0.0 copy-start.3
  1.4 1.6 copy.11.fall
  3.1 4.2 %copy.8 = bf16[8,4,132,256]{3,2,1,0:T(8,128)(2,1)} copy(bf16[8,4,132,256]{3,1,0,2:T(4,128)(2,1)} %bitcast.16) | data formatting | bytes 4325376 | tf_op jit(solution)/shard_map/transpose | solution.py:560
  7.3 0.0 copy-done
  7.3 0.0 copy-done.2
  7.3 0.0 copy-done.3
  7.3 17.6 %pack_rows.1 = (bf16[8,128,2048]{2,1,0:T(8,128)(2,1)}, bf16[8,16,1024]{2,1,0:T(8,128)(2,1)S(1)}) custom-call(bf16[132,8192]{1,0:T(8,128)(2,1)S(1)} %copy-done, s32[64,128]{1,0:T(8,128)S(1)} %bitcast.12, s32[64,128]{1,0:T(8,128)S(1)} %bitcast.13), custom_call_target="tpu_custom_call" | custom-call | tf_op jit(solution)/shard_map/pack_rows/pallas_call | solution.py:539
  24.9 0.0 copy-start.1
  24.9 0.7 copy-done.1
  25.6 135.3 %exchange_advect_settle.1 = bf16[32,132,256]{2,1,0:T(8,128)(2,1)} custom-call(bf16[8,128,2048]{2,1,0:T(8,128)(2,1)} %get-tuple-element.7.packed, bf16[8,16,1024]{2,1,0:T(8,128)(2,1)} %copy-done.1, bf16[32,132,256]{2,1,0:T(8,128)(2,1)} %bitcast.14, f32[4,8,256]{2,1,0:T(8,128)} %get-tuple-element.10.cx, f32[4,8,256]{2,1,0:T(8,128)} %get-tuple-element.9.cy, ...), custom_call_target="tpu_custom_call" | custom-call | tf_op jit(solution)/shard_map/exchange_advect_settle/pallas_call | solution.py:568
  160.9 4.2 %copy.16 = bf16[8,4,132,256]{3,1,0,2:T(4,128)(2,1)} copy(bf16[8,4,132,256]{3,2,1,0:T(8,128)(2,1)} %bitcast.15) | data formatting | bytes 4325376 | tf_op jit(solution)/shard_map/reshape | solution.py:605
  (2 shorter events, 0.0 us)
Async XLA Ops:
  1.4 5.8 %copy-start = (bf16[132,8192]{1,0:T(8,128)(2,1)S(1)}, bf16[132,8192]{1,0:T(8,128)(2,1)}, u32[]{:S(2)}) copy-start(bf16[132,8192]{1,0:T(8,128)(2,1)} %inc.1) | copy-start | bytes 6488068
  1.4 5.8 %copy-start.2 = (s32[8192,1]{0,1:T(1,128)S(1)}, s32[8192,1]{0,1:T(1,128)}, u32[]{:S(2)}) copy-start(s32[8192,1]{0,1:T(1,128)} %param.9) | copy-start | bytes 98308
  1.4 5.8 %copy-start.3 = (s32[8192]{0:T(1024)S(1)}, s32[8192]{0:T(1024)}, u32[]{:S(2)}) copy-start(s32[8192]{0:T(1024)} %param.10) | copy-start | bytes 98308
  24.9 0.7 copy-start.1
where the time goes:
time: 165 us
  Pallas kernels  153 us (93%)
  local copies, waits for them, and re-layouts  10.7 us (6%)
    pallas_call x1, Pallas kernels, per_device(): pl.pallas_call(functools.partial(main_kernel, comps, 1), out_shape=jax.Sh...  135 us
    pallas_call x1, Pallas kernels, per_device(): pl.pallas_call(functools.partial(pack_kernel, peers, capacity), out_shape...  17.6 us
    reshape x1, local copies, waits for them, and re-layouts, per_device(): settled = settled.reshape(levels, xcells, comps, ycells)  4.21 us
    transpose x1, local copies, waits for them, and re-layouts, per_device(): jnp.transpose(base_field, (1, 2, 0, 3)).reshape(groups, comps, ycells)  4.19 us

commit v1 on v0

--- a/solution.py
+++ b/solution.py
@@ -27,9 +27,12 @@
 
 
 def pack_kernel(
-    peers, capacity, inc, tiles, cells, main_out, tail_out, packed, tails, places, starts, table, sem, out_sem
+    peers, capacity, inc_in, tiles, cells, main_out, tail_out, packed, tails, inc, places, starts, table, ends,
+    totals, sem, out_sem
 ):
     comps, count = inc.shape
+    inc_copy = pltpu.make_async_copy(inc_in, inc, out_sem.at[peers])
+    inc_copy.start()
     body = comps // 16 * 16
     height = body + TAIL
     run, width = 128, 256
@@ -54,7 +57,7 @@
     bundle = min(8, peers)
 
     def rank(part, carry):
-        place, start = carry
+        place, start, end = carry
         for n in range(bundle):
             tile = part * bundle + n
             member = jnp.where(tiles[...] == tile, 1.0, 0.0)
@@ -64,35 +67,44 @@
             before = jnp.dot(above, line, preferred_element_type=jnp.float32)
             place = place + member * (inside + before - 1.0)
             start = start + jnp.where(lanes == tile, before, 0.0)
-        return place, start
+            end = end + jnp.where(
+                lanes[0:8] == tile, before[lines - 1 : lines] + line[lines - 1 : lines].astype(jnp.float32), 0.0
+            )
+        return place, start, end
 
     zero = jnp.zeros((lines, run), jnp.float32)
-    place, start = lax.fori_loop(0, peers // bundle, rank, (zero, zero))
+    place, start, end = lax.fori_loop(0, peers // bundle, rank, (zero, zero, zero[0:8]))
     places[...] = place.astype(jnp.int32) % width
     starts[...] = start.astype(jnp.int32)
+    ends[...] = end.astype(jnp.int32)
     copy = pltpu.make_async_copy(starts, table, sem)
+    end_copy = pltpu.make_async_copy(ends, totals, out_sem.at[peers + 1])
     copy.start()
+    end_copy.start()
     copy.wait()
-
-    window = lax.broadcasted_iota(jnp.int32, (width, width), 0)
+    end_copy.wait()
+
     lane = lax.broadcasted_iota(jnp.int32, (16, width), 1)
-    sub = lax.broadcasted_iota(jnp.int32, (8, width), 0)
-
-    def pair(ref, block):
-        return jnp.concatenate([ref[pl.ds(2 * block, 1)], ref[pl.ds(2 * block + 1, 1)]], axis=1)
-
-    def step(block, carry):
-        columns = pl.ds(pl.multiple_of(block * width, width), width)
-        match = one_hot(window == pair(places, block))
-        owner = pair(tiles, block)
-        cell = pair(cells, block)
+    inc_copy.wait()
+
+    def line_of(ref, line, much):
+        return jnp.concatenate([ref[pl.ds(line + n, 1)] for n in range(much)], axis=1)
+
+    def place_block(line, much):
+        size = much * run
+        columns = pl.ds(pl.multiple_of(line * run, run), size)
+        window = lax.broadcasted_iota(jnp.int32, (width, size), 0)
+        sub = lax.broadcasted_iota(jnp.int32, (8, size), 0)
+        match = one_hot(window == line_of(places, line, much))
+        owner = line_of(tiles, line, much)
+        cell = line_of(cells, line, much)
         extra = jnp.concatenate(
-            [inc[body:comps, columns].astype(jnp.float32), jnp.zeros((8 - comps + body, width), jnp.float32)],
+            [inc[body:comps, columns].astype(jnp.float32), jnp.zeros((8 - comps + body, size), jnp.float32)],
             axis=0,
         )
         extra = jnp.where(sub == 4, (cell % width).astype(jnp.float32), extra)
         extra = jnp.where(sub == 5, (cell // width).astype(jnp.float32), extra)
-        extra = jnp.concatenate([extra, jnp.zeros((8, width), jnp.float32)], axis=0)
+        extra = jnp.concatenate([extra, jnp.zeros((8, size), jnp.float32)], axis=0)
         rows = jnp.concatenate([inc[0:body, columns], extra.astype(jnp.bfloat16)], axis=0)
 
         def place_part(part, inner):
@@ -103,7 +115,7 @@
             moved = lax.dot_general(masked, match, NT, preferred_element_type=jnp.float32)
             for n in range(bundle):
                 tile = first + n
-                begin = table[2 * block, tile]
+                begin = table[line, tile]
                 chunk, low = begin // width, begin % width
                 value = moved[n * height : (n + 1) * height].astype(jnp.bfloat16)
                 now = one_hot(lane >= low)
@@ -117,9 +129,35 @@
             return inner
 
         lax.fori_loop(0, peers // bundle, place_part, 0)
+
+    much = 4
+    blocks = lines // much
+
+    def step(block, carry):
+        line = block * much
+        following = jnp.minimum(line + much, lines - 1)
+
+        def held(tile, most):
+            end = jnp.where(block == blocks - 1, totals[0, tile], table[following, tile])
+            return jnp.maximum(most, end - table[line, tile])
+
+        most = lax.fori_loop(0, peers, held, 0, unroll=bundle)
+
+        @pl.when(most <= width)
+        def _():
+            place_block(line, much)
+
+        @pl.when(most > width)
+        def _():
+            def half_block(part, inner):
+                place_block(line + 2 * part, 2)
+                return inner
+
+            lax.fori_loop(0, much // 2, half_block, 0)
+
         return carry
 
-    lax.fori_loop(0, count // width, step, 0)
+    lax.fori_loop(0, blocks, step, 0)
 
     def out_copy(tile):
         return pltpu.make_async_copy(
@@ -146,8 +184,8 @@
 
 
 def main_kernel(
-    comps, ahead, packed, tails, base_in, cx, cy, fall, out, arrived, arrived_tail, cell_of, base, total,
-    updated, advected, left, right, next_cx, flow, inflow, scale, gain, weight, face, send_sem, recv_sem,
+    comps, ahead, packed, tails, base_in, courant_x, courant_y, fall_in, out, arrived, arrived_tail, cell_of, base, total,
+    updated, advected, left, right, next_cx, flow, inflow, entry, scale, gain, weight, face, cx, cy, send_sem, recv_sem,
     halo_send, halo_recv, face_send, face_recv, flow_send, flow_recv, own_sem,
 ):
     peers, body, capacity = packed.shape
@@ -165,6 +203,14 @@
     own_tail.start()
     own_main.start()
     base_copy.start()
+
+    inner = (lax.broadcasted_iota(jnp.int32, (1, width), 1) > 0).astype(jnp.float32)
+    for k in range(levels):
+        along_x, along_y = courant_x[k].astype(jnp.float32), courant_y[k].astype(jnp.float32)
+        for i in range(xcells):
+            row = along_x[i : i + 1]
+            cx[i, k : k + 1] = jnp.where(has_prev, row, 0.0) if i == 0 else row
+            cy[i, k : k + 1] = along_y[i : i + 1] * inner
 
     barrier = pltpu.get_barrier_semaphore()
 
@@ -234,6 +280,7 @@
         right[...] = jnp.zeros_like(right)
         next_cx[...] = jnp.zeros_like(next_cx)
 
+    fall = jnp.transpose(fall_in[...])
     column = lax.broadcasted_iota(jnp.int32, (1, fall.shape[1]), 1)
 
     def along(values, at):
@@ -409,7 +456,7 @@
             none = tuple(jnp.zeros((16, width), jnp.float32) for _ in chosen)
             flows = lax.fori_loop(0, levels, level, none, unroll=2)
             for i, flowing in zip(chosen, flows):
-                flow[i, span] = flowing
+                flow[i, span] = flowing.astype(jnp.bfloat16)
 
         inner = list(range(1, xcells - 1))
         for span in spans(number):
@@ -436,17 +483,20 @@
         def _():
             for i in range(xcells):
                 for span in spans(number):
-                    inflow[0, i, span] = jnp.zeros((16, width), jnp.float32)
+                    entry[i, span] = jnp.zeros((16, width), jnp.float32)
 
         for d in range(1, slabs):
 
             @pl.when(slab + d < slabs)
             def _(d=d):
                 flow_copy(number, d).wait_recv()
-                if d > 1:
-                    for i in range(xcells):
-                        for span in spans(number):
-                            inflow[0, i, span] += wide(weight[d - 1, span]) * inflow[d - 1, i, span]
+                for i in range(xcells):
+                    for span in spans(number):
+                        came = inflow[d - 1, i, span].astype(jnp.float32)
+                        if d == 1:
+                            entry[i, span] = came
+                        else:
+                            entry[i, span] += wide(weight[d - 1, span]) * came
 
         for span in spans(number):
             filled = min(comps, span.stop) - span.start
@@ -462,7 +512,7 @@
                     result.append(value * kept)
                 return tuple(result)
 
-            start = tuple(inflow[0, i, span] for i in range(xcells))
+            start = tuple(entry[i, span] for i in range(xcells))
             lax.fori_loop(0, levels, level, start, unroll=2)
 
     own_tail.wait()
@@ -542,29 +592,25 @@
             jax.ShapeDtypeStruct((peers, body, capacity), jnp.bfloat16),
             jax.ShapeDtypeStruct((peers, TAIL, capacity // 2), jnp.bfloat16),
         ),
-        in_specs=[vmem] * 3,
+        in_specs=[anywhere, vmem, vmem],
         out_specs=(anywhere, anywhere),
         scratch_shapes=[
-            pltpu.VMEM((peers, height, capacity + 256), jnp.bfloat16),
+            pltpu.VMEM((peers, height, capacity + 512), jnp.bfloat16),
             pltpu.VMEM((peers, TAIL, capacity // 2), jnp.bfloat16),
+            pltpu.VMEM((comps, row_count), jnp.bfloat16),
             pltpu.VMEM((lines, 128), jnp.int32),
             pltpu.VMEM((lines, 128), jnp.int32),
             pltpu.SMEM((lines, 128), jnp.int32),
+            pltpu.VMEM((8, 128), jnp.int32),
+            pltpu.SMEM((8, 128), jnp.int32),
             pltpu.SemaphoreType.DMA,
-            pltpu.SemaphoreType.DMA((peers,)),
+            pltpu.SemaphoreType.DMA((peers + 2,)),
         ],
         compiler_params=pltpu.CompilerParams(vmem_limit_bytes=48 * 2**20),
         name="pack_rows",
     )(increments, dest_tile.reshape(lines, 128), dest_cell.reshape(lines, 128))
 
     base = jnp.transpose(base_field, (1, 2, 0, 3)).reshape(groups, comps, ycells)
-    first = jnp.logical_and(
-        lax.axis_index("xy") == 0, jnp.arange(xcells)[:, None, None] == 0
-    )
-    face_x = jnp.where(first, 0.0, jnp.transpose(courant_x.astype(jnp.float32), (1, 0, 2)))
-    face_y = jnp.transpose(courant_y.astype(jnp.float32), (1, 0, 2))
-    face_y = jnp.where(jnp.arange(ycells)[None, None, :] == 0, 0.0, face_y)
-
     settled = pl.pallas_call(
         functools.partial(main_kernel, comps, 1),
         out_shape=jax.ShapeDtypeStruct((groups, comps, ycells), jnp.bfloat16),
@@ -581,12 +627,15 @@
             pltpu.VMEM((levels, height, ycells), jnp.bfloat16),
             pltpu.VMEM((levels, height, ycells), jnp.bfloat16),
             pltpu.VMEM((levels, ycells), jnp.float32),
+            pltpu.VMEM((xcells, height, ycells), jnp.bfloat16),
+            pltpu.VMEM((slabs - 1, xcells, height, ycells), jnp.bfloat16),
             pltpu.VMEM((xcells, height, ycells), jnp.float32),
-            pltpu.VMEM((slabs - 1, xcells, height, ycells), jnp.float32),
             pltpu.VMEM((levels, height, 128), jnp.float32),
             pltpu.VMEM((levels, height, 128), jnp.float32),
             pltpu.VMEM((slabs - 1, height, 128), jnp.float32),
             pltpu.VMEM((5, xcells, levels, ycells), jnp.float32),
+            pltpu.VMEM((xcells, levels, ycells), jnp.float32),
+            pltpu.VMEM((xcells, levels, ycells), jnp.float32),
             pltpu.SemaphoreType.DMA((count, peers)),
             pltpu.SemaphoreType.DMA((count, peers)),
             pltpu.SemaphoreType.DMA((count, 2)),
@@ -601,7 +650,7 @@
             vmem_limit_bytes=56 * 2**20, collective_id=0, has_side_effects=True
         ),
         name="exchange_advect_settle",
-    )(packed, tails, base, face_x, face_y, fall_courant)
+    )(packed, tails, base, courant_x, courant_y, jnp.transpose(fall_courant))
     settled = settled.reshape(levels, xcells, comps, ycells)
     return jnp.transpose(settled, (2, 0, 1, 3))
 

time: 165 us -> 158 us (0.958)
  Pallas kernels: 153 us -> 148 us
    pallas_call x1, Pallas kernels: 17.6 us -> 13.7 us  [per_device(): pl.pallas_call(functools.partial(pack_kernel, peers, capacity), out_shape...]
where the time goes in v1:
time: 158 us; the launch traced here: 157 us
  Pallas kernels  148 us (94%)
  local copies, waits for them, and re-layouts  9.25 us (6%)
    pallas_call x1, Pallas kernels, per_device(): pl.pallas_call(functools.partial(main_kernel, comps, 1), out_shape=jax.Sh...  134 us
    pallas_call x1, Pallas kernels, per_device(): pl.pallas_call(functools.partial(pack_kernel, peers, capacity), out_shape...  13.7 us
    transpose x1, local copies, waits for them, and re-layouts, per_device(): jnp.transpose(base_field, (1, 2, 0, 3)).reshape(groups, comps, ycells)  4.33 us
    reshape x1, local copies, waits for them, and re-layouts, per_device(): settled = settled.reshape(levels, xcells, comps, ycells)  4.21 us

profile of v1, /device:TPU:0, one launch (start us, length us, event | category | flops | bytes accessed | tf_op | source)
XLA Modules:
  0.0 157.3 jit_solution(18024729383069008134)
XLA Ops:
  0.0 0.0 copy-start.3
  0.0 0.0 copy-start.2
  0.0 0.0 copy-start
  0.0 4.3 %copy.8 = bf16[8,4,132,256]{3,2,1,0:T(8,128)(2,1)} copy(bf16[8,4,132,256]{3,1,0,2:T(4,128)(2,1)} %bitcast.13) | data formatting | bytes 4325376 | tf_op jit(solution)/shard_map/transpose | solution.py:613
  4.3 0.0 copy-done.3
  4.3 0.0 copy-done.2
  4.3 0.0 copy-done
  4.3 13.7 %pack_rows.1 = (bf16[8,128,2048]{2,1,0:T(8,128)(2,1)}, bf16[8,16,1024]{2,1,0:T(8,128)(2,1)S(1)}) custom-call(bf16[132,8192]{1,0:T(8,128)(2,1)S(1)} %copy-done, s32[64,128]{1,0:T(8,128)S(1)} %bitcast.9, s32[64,128]{1,0:T(8,128)S(1)} %bitcast.10), custom_call_target="tpu_custom_call" | custom-call | tf_op jit(solution)/shard_map/pack_rows/pallas_call | solution.py:589
  18.0 0.0 copy-start.1
  18.1 0.7 copy-done.1
  18.7 134.4 %exchange_advect_settle.1 = bf16[32,132,256]{2,1,0:T(8,128)(2,1)} custom-call(bf16[8,128,2048]{2,1,0:T(8,128)(2,1)} %get-tuple-element.7.packed, bf16[8,16,1024]{2,1,0:T(8,128)(2,1)} %copy-done.1, bf16[32,132,256]{2,1,0:T(8,128)(2,1)} %bitcast.11, bf16[8,4,256]{2,1,0:T(4,128)(2,1)} %courant_x.1, bf16[8,4,256]{2,1,0:T(4,128)(2,1)} %courant_y.1, ...), custom_call_target="tpu_custom_call" | custom-call | tf_op jit(solution)/shard_map/exchange_advect_settle/pallas_call | solution.py:614
  153.1 4.2 %copy.11 = bf16[8,4,132,256]{3,1,0,2:T(4,128)(2,1)} copy(bf16[8,4,132,256]{3,2,1,0:T(8,128)(2,1)} %bitcast.12) | data formatting | bytes 4325376 | tf_op jit(solution)/shard_map/reshape | solution.py:654
Async XLA Ops:
  0.0 4.3 %copy-start.3 = (s32[8192]{0:T(1024)S(1)}, s32[8192]{0:T(1024)}, u32[]{:S(2)}) copy-start(s32[8192]{0:T(1024)} %param.10) | copy-start | bytes 98308
  0.0 4.3 %copy-start.2 = (s32[8192,1]{0,1:T(1,128)S(1)}, s32[8192,1]{0,1:T(1,128)}, u32[]{:S(2)}) copy-start(s32[8192,1]{0,1:T(1,128)} %param.9) | copy-start | bytes 98308
  0.0 4.3 %copy-start = (bf16[132,8192]{1,0:T(8,128)(2,1)S(1)}, bf16[132,8192]{1,0:T(8,128)(2,1)}, u32[]{:S(2)}) copy-start(bf16[132,8192]{1,0:T(8,128)(2,1)} %inc_in.1) | copy-start | bytes 6488068
  18.0 0.7 copy-start.1

commit v2 on v1

--- a/solution.py
+++ b/solution.py
@@ -20,7 +20,7 @@
     parts = [(body, TAIL)]
     first = 0
     while first < body:
-        rows = 16 if body - first <= 32 else 32
+        rows = 16 if first == 0 or body - first < 48 else 32
         parts.append((first, rows))
         first += rows
     return parts
@@ -128,12 +128,15 @@
                 packed[tile, :, there] = value * later
             return inner
 
-        lax.fori_loop(0, peers // bundle, place_part, 0)
+        if peers == bundle:
+            place_part(0, 0)
+        else:
+            lax.fori_loop(0, peers // bundle, place_part, 0)
 
     much = 4
     blocks = lines // much
 
-    def step(block, carry):
+    def most_held(block, most):
         line = block * much
         following = jnp.minimum(line + much, lines - 1)
 
@@ -141,23 +144,25 @@
             end = jnp.where(block == blocks - 1, totals[0, tile], table[following, tile])
             return jnp.maximum(most, end - table[line, tile])
 
-        most = lax.fori_loop(0, peers, held, 0, unroll=bundle)
-
-        @pl.when(most <= width)
-        def _():
-            place_block(line, much)
-
-        @pl.when(most > width)
-        def _():
-            def half_block(part, inner):
-                place_block(line + 2 * part, 2)
-                return inner
-
-            lax.fori_loop(0, much // 2, half_block, 0)
-
-        return carry
-
-    lax.fori_loop(0, blocks, step, 0)
+        return lax.fori_loop(0, peers, held, most, unroll=bundle)
+
+    most = lax.fori_loop(0, blocks, most_held, 0)
+
+    @pl.when(most <= width)
+    def _():
+        def step(block, carry):
+            place_block(block * much, much)
+            return carry
+
+        lax.fori_loop(0, blocks, step, 0, unroll=4)
+
+    @pl.when(most > width)
+    def _():
+        def step(block, carry):
+            place_block(block * 2, 2)
+            return carry
+
+        lax.fori_loop(0, lines // 2, step, 0)
 
     def out_copy(tile):
         return pltpu.make_async_copy(
@@ -184,7 +189,7 @@
 
 
 def main_kernel(
-    comps, ahead, packed, tails, base_in, courant_x, courant_y, fall_in, out, arrived, arrived_tail, cell_of, base, total,
+    comps, ahead, packed, tails, base_in, courant_x, courant_y, fall_in, out, arrived, arrived_tail, cell_of, base, lifted, total,
     updated, advected, left, right, next_cx, flow, inflow, entry, scale, gain, weight, face, cx, cy, send_sem, recv_sem,
     halo_send, halo_recv, face_send, face_recv, flow_send, flow_recv, own_sem,
 ):
@@ -321,6 +326,24 @@
     def wide(value):
         return jnp.concatenate([value] * (width // 128), axis=1)
 
+    def lift(number):
+        first, rows = stages[number]
+        filled = min(comps, first + rows) - first
+
+        def component(b, carry):
+            for k in range(levels):
+                value = base[first + b, k].astype(jnp.float32)
+                for part in range(width // 128):
+                    lifted[part, pl.ds(k * xcells * rows + b, xcells, stride=rows)] = value[
+                        :, part * 128 : (part + 1) * 128
+                    ]
+            return carry
+
+        lax.fori_loop(0, filled, component, 0)
+
+    def lifted_at(at, rows):
+        return jnp.concatenate([lifted[part, pl.ds(at, rows)] for part in range(width // 128)], axis=1)
+
     def add_rows(number, step, begin):
         first, rows = stages[number]
         bundle = min(groups, 1024 // rows)
@@ -343,9 +366,9 @@
             sums = lax.dot_general(masked, match, NT, preferred_element_type=jnp.float32)
             sums = sums.reshape(bundle, rows, width)
             if begin and number > 0:
-                total[pl.ds(at, bundle), first : first + rows] = sums + base[
-                    pl.ds(at, bundle), first : first + rows
-                ].astype(jnp.float32)
+                for n in range(bundle):
+                    spot = pl.multiple_of((at + n) * rows, rows)
+                    total[at + n, first : first + rows] = sums[n] + lifted_at(spot, rows)
             elif begin:
                 total[pl.ds(at, bundle), first : first + rows] = sums
             else:
@@ -376,7 +399,8 @@
             if number == 0:
                 value = jnp.concatenate(
                     [
-                        value[: comps - body] + base[counter, body:comps].astype(jnp.float32),
+                        value[: comps - body]
+                        + lifted_at(pl.multiple_of(counter * rows, rows), 8)[: comps - body],
                         jnp.zeros((rows - comps + body, width), jnp.float32),
                     ],
                     axis=0,
@@ -523,9 +547,11 @@
         if number == 1:
             own_main.wait()
             base_copy.wait()
+            lift(0)
+            finish(0)
+        if number > 0:
+            lift(number)
         add_rows(number, 0, True)
-        if number == 1:
-            finish(0)
 
         def receive(order, carry):
             step = turn(order)
@@ -606,11 +632,10 @@
             pltpu.SemaphoreType.DMA,
             pltpu.SemaphoreType.DMA((peers + 2,)),
         ],
-        compiler_params=pltpu.CompilerParams(vmem_limit_bytes=48 * 2**20),
+        compiler_params=pltpu.CompilerParams(vmem_limit_bytes=62 * 2**20),
         name="pack_rows",
     )(increments, dest_tile.reshape(lines, 128), dest_cell.reshape(lines, 128))
 
-    base = jnp.transpose(base_field, (1, 2, 0, 3)).reshape(groups, comps, ycells)
     settled = pl.pallas_call(
         functools.partial(main_kernel, comps, 1),
         out_shape=jax.ShapeDtypeStruct((groups, comps, ycells), jnp.bfloat16),
@@ -620,7 +645,8 @@
             pltpu.VMEM((peers, body, capacity), jnp.bfloat16),
             pltpu.VMEM((peers, TAIL, capacity // 2), jnp.bfloat16),
             pltpu.VMEM((peers, 8, capacity), jnp.float32),
-            pltpu.VMEM((groups, comps, ycells), jnp.bfloat16),
+            pltpu.VMEM((comps, levels, xcells, ycells), jnp.bfloat16),
+            pltpu.VMEM((2, groups * 32, 128), jnp.float32),
             pltpu.VMEM((groups, height, ycells), jnp.float32),
             pltpu.VMEM((xcells, levels, height, ycells), jnp.bfloat16),
             pltpu.VMEM((xcells, levels, height, ycells), jnp.bfloat16),
@@ -650,7 +676,7 @@
             vmem_limit_bytes=56 * 2**20, collective_id=0, has_side_effects=True
         ),
         name="exchange_advect_settle",
-    )(packed, tails, base, courant_x, courant_y, jnp.transpose(fall_courant))
+    )(packed, tails, base_field, courant_x, courant_y, jnp.transpose(fall_courant))
     settled = settled.reshape(levels, xcells, comps, ycells)
     return jnp.transpose(settled, (2, 0, 1, 3))
 

time: 158 us -> 150 us (0.949)
  local copies, waits for them, and re-layouts: 9.25 us -> 4.21 us
  Pallas kernels: 148 us -> 145 us
    transpose x1 -> x0, local copies, waits for them, and re-layouts: 4.33 us -> none  [per_device(): jnp.transpose(base_field, (1, 2, 0, 3)).reshape(groups, comps, ycells)]
    pallas_call x1, Pallas kernels: 134 us -> 132 us  [per_device(): pl.pallas_call(functools.partial(main_kernel, comps, 1), out_shape=jax.Sh...]
where the time goes in v2:
time: 150 us; the launch traced here: 149 us
  Pallas kernels  145 us (97%)
  local copies, waits for them, and re-layouts  4.21 us (3%)
    pallas_call x1, Pallas kernels, per_device(): pl.pallas_call(functools.partial(main_kernel, comps, 1), out_shape=jax.Sh...  132 us
    pallas_call x1, Pallas kernels, per_device(): pl.pallas_call(functools.partial(pack_kernel, peers, capacity), out_shape...  12.9 us
    reshape x1, local copies, waits for them, and re-layouts, per_device(): settled = settled.reshape(levels, xcells, comps, ycells)  4.21 us

profile of v2, /device:TPU:0, one launch (start us, length us, event | category | flops | bytes accessed | tf_op | source)
XLA Modules:
  0.0 149.3 jit_solution(12817189853969061896)
XLA Ops:
  0.0 12.9 %pack_rows.1 = (bf16[8,128,2048]{2,1,0:T(8,128)(2,1)}, bf16[8,16,1024]{2,1,0:T(8,128)(2,1)}) custom-call(bf16[132,8192]{1,0:T(8,128)(2,1)} %inc_in.1, s32[64,128]{1,0:T(8,128)} %bitcast.8, s32[64,128]{1,0:T(8,128)} %bitcast.9), custom_call_target="tpu_custom_call" | custom-call | tf_op jit(solution)/shard_map/pack_rows/pallas_call | solution.py:615
  12.9 132.2 %exchange_advect_settle.1 = bf16[32,132,256]{2,1,0:T(8,128)(2,1)} custom-call(bf16[8,128,2048]{2,1,0:T(8,128)(2,1)} %get-tuple-element.7.packed, bf16[8,16,1024]{2,1,0:T(8,128)(2,1)} %get-tuple-element.8.tails, bf16[132,8,4,256]{3,2,1,0:T(4,128)(2,1)} %base_in.1, bf16[8,4,256]{2,1,0:T(4,128)(2,1)} %courant_x.1, bf16[8,4,256]{2,1,0:T(4,128)(2,1)} %courant_y.1, ...), custom_call_target="tpu_custom_call" | custom-call | tf_op jit(solution)/shard_map/exchange_advect_settle/pallas_call | solution.py:639
  145.1 4.2 %copy.10 = bf16[8,4,132,256]{3,1,0,2:T(4,128)(2,1)} copy(bf16[8,4,132,256]{3,2,1,0:T(8,128)(2,1)} %bitcast.7) | data formatting | bytes 4325376 | tf_op jit(solution)/shard_map/reshape | solution.py:680

commit v3 on v2

--- a/solution.py
+++ b/solution.py
@@ -542,8 +542,6 @@
     own_tail.wait()
     faces()
     for number in range(len(stages)):
-        if number + ahead < len(stages):
-            start_rows(number + ahead)
         if number == 1:
             own_main.wait()
             base_copy.wait()
@@ -560,7 +558,10 @@
             return carry
 
         middle = (peers - 1) // 2
-        lax.fori_loop(0, middle, receive, 0)
+        lax.fori_loop(0, 2, receive, 0)
+        if number + ahead < len(stages):
+            start_rows(number + ahead)
+        lax.fori_loop(2, middle, receive, 0)
         if number > 1:
             settle(number - 2)
         lax.fori_loop(middle, peers - 1, receive, 0)

time: 150 us -> 147 us (0.980)
  Pallas kernels: 145 us -> 142 us
    pallas_call x1, Pallas kernels: 132 us -> 129 us  [per_device(): pl.pallas_call(functools.partial(main_kernel, comps, 1), out_shape=jax.Sh...]
where the time goes in v3:
time: 147 us; the launch traced here: 146 us
  Pallas kernels  142 us (97%)
  local copies, waits for them, and re-layouts  4.21 us (3%)
    pallas_call x1, Pallas kernels, per_device(): pl.pallas_call(functools.partial(main_kernel, comps, 1), out_shape=jax.Sh...  129 us
    pallas_call x1, Pallas kernels, per_device(): pl.pallas_call(functools.partial(pack_kernel, peers, capacity), out_shape...  12.9 us
    reshape x1, local copies, waits for them, and re-layouts, per_device(): settled = settled.reshape(levels, xcells, comps, ycells)  4.21 us

profile of v3, /device:TPU:0, one launch (start us, length us, event | category | flops | bytes accessed | tf_op | source)
XLA Modules:
  0.0 146.2 jit_solution(2965280720021094719)
XLA Ops:
  0.0 12.9 %pack_rows.1 = (bf16[8,128,2048]{2,1,0:T(8,128)(2,1)}, bf16[8,16,1024]{2,1,0:T(8,128)(2,1)}) custom-call(bf16[132,8192]{1,0:T(8,128)(2,1)} %inc_in.1, s32[64,128]{1,0:T(8,128)} %bitcast.8, s32[64,128]{1,0:T(8,128)} %bitcast.9), custom_call_target="tpu_custom_call" | custom-call | tf_op jit(solution)/shard_map/pack_rows/pallas_call | solution.py:616
  12.9 129.1 %exchange_advect_settle.1 = bf16[32,132,256]{2,1,0:T(8,128)(2,1)} custom-call(bf16[8,128,2048]{2,1,0:T(8,128)(2,1)} %get-tuple-element.7.packed, bf16[8,16,1024]{2,1,0:T(8,128)(2,1)} %get-tuple-element.8.tails, bf16[132,8,4,256]{3,2,1,0:T(4,128)(2,1)} %base_in.1, bf16[8,4,256]{2,1,0:T(4,128)(2,1)} %courant_x.1, bf16[8,4,256]{2,1,0:T(4,128)(2,1)} %courant_y.1, ...), custom_call_target="tpu_custom_call" | custom-call | tf_op jit(solution)/shard_map/exchange_advect_settle/pallas_call | solution.py:640
  142.0 4.2 %copy.10 = bf16[8,4,132,256]{3,1,0,2:T(4,128)(2,1)} copy(bf16[8,4,132,256]{3,2,1,0:T(8,128)(2,1)} %bitcast.7) | data formatting | bytes 4325376 | tf_op jit(solution)/shard_map/reshape | solution.py:681

commit v4 on v3

--- a/solution.py
+++ b/solution.py
@@ -154,7 +154,7 @@
             place_block(block * much, much)
             return carry
 
-        lax.fori_loop(0, blocks, step, 0, unroll=4)
+        lax.fori_loop(0, blocks, step, 0, unroll=8)
 
     @pl.when(most > width)
     def _():

time: 147 us -> 146 us (level)
  no operation moved by 1% of the time
where the time goes in v4:
time: 146 us
  Pallas kernels  142 us (97%)
  local copies, waits for them, and re-layouts  4.21 us (3%)
    pallas_call x1, Pallas kernels, per_device(): pl.pallas_call(functools.partial(main_kernel, comps, 1), out_shape=jax.Sh...  129 us
    pallas_call x1, Pallas kernels, per_device(): pl.pallas_call(functools.partial(pack_kernel, peers, capacity), out_shape...  12.7 us
    reshape x1, local copies, waits for them, and re-layouts, per_device(): settled = settled.reshape(levels, xcells, comps, ycells)  4.21 us

profile of v4, /device:TPU:0, one launch (start us, length us, event | category | flops | bytes accessed | tf_op | source)
XLA Modules:
  0.0 145.9 jit_solution(2760728752262110944)
XLA Ops:
  0.0 12.7 %pack_rows.1 = (bf16[8,128,2048]{2,1,0:T(8,128)(2,1)}, bf16[8,16,1024]{2,1,0:T(8,128)(2,1)}) custom-call(bf16[132,8192]{1,0:T(8,128)(2,1)} %inc_in.1, s32[64,128]{1,0:T(8,128)} %bitcast.8, s32[64,128]{1,0:T(8,128)} %bitcast.9), custom_call_target="tpu_custom_call" | custom-call | tf_op jit(solution)/shard_map/pack_rows/pallas_call | solution.py:616
  12.7 129.1 %exchange_advect_settle.1 = bf16[32,132,256]{2,1,0:T(8,128)(2,1)} custom-call(bf16[8,128,2048]{2,1,0:T(8,128)(2,1)} %get-tuple-element.7.packed, bf16[8,16,1024]{2,1,0:T(8,128)(2,1)} %get-tuple-element.8.tails, bf16[132,8,4,256]{3,2,1,0:T(4,128)(2,1)} %base_in.1, bf16[8,4,256]{2,1,0:T(4,128)(2,1)} %courant_x.1, bf16[8,4,256]{2,1,0:T(4,128)(2,1)} %courant_y.1, ...), custom_call_target="tpu_custom_call" | custom-call | tf_op jit(solution)/shard_map/exchange_advect_settle/pallas_call | solution.py:640
  141.7 4.2 %copy.10 = bf16[8,4,132,256]{3,1,0,2:T(4,128)(2,1)} copy(bf16[8,4,132,256]{3,2,1,0:T(8,128)(2,1)} %bitcast.7) | data formatting | bytes 4325376 | tf_op jit(solution)/shard_map/reshape | solution.py:681
